TPU v7x, 128 devices: a whole 4x4x4 slice. The times are simulated.
128 devices in a mesh: section: 8 (over y, core), dp: 16 (over z, x).
Axes of the slice: x: 4, y: 4, z: 4, core: 2. Of those that a mesh axis runs over, the one named last changes fastest.
Arguments:
- hidden: bfloat16 [4, 576, 8192], P(None, 'dp'), may hold values from -6 to 6
- lengths: int32 [4, 16], replicated, may hold values from 1 to 36, 256 in all within a row
- response_mask: int32 [4, 576], replicated, may hold values 0 or 1
- norm_gain: float32 [8, 8192], P('section'), may hold values from 0.25 to 1.75
- weight_in: bfloat16 [8, 8192, 256], P('section'), may hold values from -0.0625 to 0.0625
- weight_out: bfloat16 [8, 256, 8192], P('section'), may hold values from -0.375 to 0.375
- final_gain: float32 [8192], replicated, may hold values from 0.25 to 1.75
- value_heads: float32 [3, 8192], replicated, may hold values from -0.0625 to 0.0625
- old_values: float32 [3, 4, 576], replicated, may hold values from -6 to 6
- advantages: float32 [3, 4, 576], replicated, may hold values from -6 to 6
- multipliers: float32 [2], replicated, may hold values from 0.5 to 4
Outputs:
- grad_in: float32 [8, 8192, 256], P('section', 'dp')
- grad_out: float32 [8, 256, 8192], P('section', None, 'dp')
- objective: float32 [], replicated
Inputs may be any that keep to these rules, and one draw needn't show every extreme that they name: In every micro-batch the 16 lengths sum to 256 and the longest equals 36.
All inputs are finite; a program needn't handle non-finite values.
Results may differ from a plain program's by a relative error of at most 0.034.
Values may be sent and summed in bfloat16 or wider, within the bound.
A program may use at most 128 MiB of HBM per device.

v0:
```python
import functools

import jax
import jax.numpy as jnp
from jax import lax
from jax.experimental import pallas as pl
from jax.experimental.pallas import tpu as pltpu
from jax.sharding import PartitionSpec as P

EPS = 1e-05
LOSS_SCALE = 4096.0
BAL = 16

f32 = jnp.float32
bf16 = jnp.bfloat16
NT = (((1,), (1,)), ((), ()))
TN = (((0,), (0,)), ((), ()))
NN = (((1,), (0,)), ((), ()))
MESH = pl.DeviceIdType.MESH
SIDE = 4
COPIES = 288


def mm(a, b, dims=NN):
    return lax.dot_general(a, b, dims, preferred_element_type=f32)


def exact(a, b, dims):
    return lax.dot_general(
        a, b, dims, precision=lax.Precision.HIGHEST, preferred_element_type=f32
    )


def split(v, terms):
    out = []
    for _ in range(terms):
        hi = v.astype(bf16)
        out.append(hi)
        v = v - hi.astype(f32)
    return out

def kernel(
    layers,
    width,
    grad_scale,
    win_ref,
    wout_ref,
    gw_ref,
    gain_ref,
    x0_ref,
    put_ref,
    sel_ref,
    side_ref,
    place_ref,
    head_ref,
    scale_ref,
    grad_in_ref,
    grad_out_ref,
    loss_ref,
    win,
    wout,
    sums,
    wo_all,
    gw_all,
    x_all,
    x_sel,
    pay,
    rb,
    tp,
    r1,
    s1,
    r2,
    held,
    rr,
    sb,
    rq,
    mine,
    other,
    block,
    sums_t,
    send_sem,
    recv_sem,
    local_sem,
):
    s = lax.axis_index("section")
    d = lax.axis_index("dp")
    y, c = s // 2, s % 2
    z, x = d // SIDE, d % SIDE
    me = {"x": x, "y": y, "z": z}
    shards = SIDE * SIDE
    part, adapt = gw_ref.shape
    heads = 3
    rows = put_ref.shape[1]
    step = lambda a, off: (me[a] + off + SIDE) % SIDE

    def peer(axis, off):
        if axis == "x":
            return {"section": s, "dp": z * SIDE + step("x", off)}
        if axis == "z":
            return {"section": s, "dp": step("z", off) * SIDE + x}
        return {"section": step("y", off) * 2 + c, "dp": d}

    twin = {"section": y * 2 + (1 - c), "dp": d}

    def shard_at(off):
        return (d + off + shards) % shards

    def layer_at(off):
        return (s + off + layers) % layers

    barrier = pltpu.get_barrier_semaphore()
    for off in range(1, shards):
        pl.semaphore_signal(
            barrier, inc=1, device_id={"section": s, "dp": shard_at(off)}, device_id_type=MESH
        )
    for off in range(1, layers):
        pl.semaphore_signal(
            barrier, inc=1, device_id={"section": layer_at(off), "dp": d}, device_id_type=MESH
        )
    pl.semaphore_wait(barrier, shards + layers - 2)

    issued = []
    count = [0, 0]

    def new():
        count[0] += 1
        return count[0] - 1

    def remote(src, dst, at, to):
        return pltpu.make_async_remote_copy(
            src_ref=src,
            dst_ref=dst,
            send_sem=send_sem.at[at],
            recv_sem=recv_sem.at[at],
            device_id=to,
            device_id_type=MESH,
        )

    def send(src, dst, at, to):
        copy = remote(src, dst, at, to)
        copy.start()
        issued.append(copy)

    def arrived(dst, at):
        remote(dst, dst, at, twin).wait_recv()

    def local(src, dst):
        count[1] += 1
        copy = pltpu.make_async_copy(src, dst, local_sem.at[count[1] - 1])
        copy.start()
        return copy

    class Ring:
        def __init__(self, axis, slab, swaps=False):
            self.slab = slab
            self.ids = [new() for _ in range(6)]
            self.plus, self.minus = peer(axis, 1), peer(axis, -1)
            self.swaps = {}
            if swaps:
                for v in (0, -1, 1, 2):
                    for h in (0, 1):
                        self.swaps[v, h] = new()

        def send(self, v, h, n, to):
            ref = self.slab(v, h, c)
            send(ref, ref, self.ids[n], to)

        def wait(self, v, h, n):
            arrived(self.slab(v, h, c), self.ids[n])
            self.swap(v, h)

        def swap(self, v, h):
            if self.swaps:
                ref = self.slab(v, h, c)
                send(ref, ref, self.swaps[v, h], twin)

        def start(self):
            self.send(0, 0, 0, self.plus)
            self.send(0, 1, 2, self.minus)
            self.send(0, 1, 1, self.plus)
            self.send(0, 0, 3, self.minus)
            self.swap(0, 0)
            self.swap(0, 1)

        def relay(self):
            arrived(self.slab(-1, 0, c), self.ids[0])
            self.send(-1, 0, 4, self.plus)
            arrived(self.slab(1, 1, c), self.ids[2])
            self.send(1, 1, 5, self.minus)
            self.swap(-1, 0)
            self.swap(1, 1)

        def finish(self):
            self.wait(-1, 1, 1)
            self.wait(1, 0, 3)
            self.wait(2, 0, 4)
            self.wait(2, 1, 5)

        def twins(self):
            for (v, h), at in self.swaps.items():
                arrived(self.slab(v, h, 1 - c), at)

    def gather(at, columns, meanwhile=None):
        third = (columns // 384) * 128
        bounds = [0, third, 2 * third, columns]
        orders = [("x", "z", "y"), ("z", "y", "x"), ("y", "x", "z")]
        for phase in range(3):
            rings = []
            for p, order in enumerate(orders):
                lo, hi = bounds[p], bounds[p + 1]
                mid = lo + ((hi - lo) // 256) * 128
                cuts = [(lo, mid - lo), (mid, hi - mid)]

                def slab(v, h, core, order=order, cuts=cuts):
                    where = dict(me)
                    for a in order[:phase]:
                        where[a] = pl.ds(0, SIDE)
                    where[order[phase]] = step(order[phase], v)
                    return at(where, core, pl.ds(*cuts[h]))

                rings.append(Ring(order[phase], slab, swaps=phase == 2))
            for ring in rings:
                ring.start()
            if phase == 2 and meanwhile is not None:
                meanwhile()
            for ring in rings:
                ring.relay()
            for ring in rings:
                ring.finish()
        for ring in rings:
            ring.twins()

    chunks = win.shape[0]
    loads = []
    for k in range(chunks):
        loads.append(local(win_ref.at[pl.ds(k * part, part)], win.at[k]))
        loads.append(local(wout_ref.at[:, pl.ds(k * part, part)], wout.at[k]))

    half = adapt // 2
    wo_ring = Ring(
        "y", lambda v, h, core: wo_all.at[step("y", v), core, pl.ds(h * half, half)], True
    )
    columns = pl.ds(pl.multiple_of(d * part, part), part)
    local(wout_ref.at[:, columns], wo_all.at[y, c]).wait()
    wo_ring.start()
    wide = part // 2
    keep = []
    for h in (0, 1):
        keep.append(
            local(
                x0_ref.at[:rows, pl.ds(pl.multiple_of(d * part + h * wide, wide), wide)],
                x_all.at[h, d],
            )
        )
    x_ids = [new() for _ in range(shards)]
    x_swaps = [new() for _ in range(shards)]
    for off in range(1, shards):
        to = shard_at(off)
        send(
            x0_ref.at[:rows, pl.ds(pl.multiple_of(to * part + c * wide, wide), wide)],
            x_all.at[c, d],
            x_ids[off],
            {"section": s, "dp": to},
        )
    long = part // 2
    gw_ring = Ring(
        "y", lambda v, h, core: gw_all.at[step("y", v), core, pl.ds(h * long, long)], True
    )
    gw_all[y, c] = gw_ref[...]

    square = jnp.zeros((rows, 128), f32)
    for copy in loads:
        copy.wait()
    sums[...] = jnp.zeros(sums.shape, f32)

    def chunk(k, square):
        cut = pl.ds(pl.multiple_of(k * part, part), part)
        both = x0_ref[:, cut]
        x = both[:rows].astype(f32)
        for i in range(part // 128):
            piece = x[:, i * 128 : (i + 1) * 128]
            square = square + piece * piece
        gained = (x * gain_ref[:, cut]).astype(bf16)
        sums[:rows, :adapt] += mm(gained, win[k])
        sums[:, adapt : 2 * adapt] += mm(both, wout[k], NT)
        sums[:rows, 2 * adapt :] += mm(both[:rows], both[rows:], NT)
        return square

    square = jnp.sum(lax.fori_loop(0, chunks, chunk, square), axis=1, keepdims=True)
    heads_by = [rows + 3 * h for h in range(heads)]
    est = sums[:rows, 2 * adapt :]
    lane = lax.broadcasted_iota(jnp.int32, (rows, 128), 1)
    dots = [square]
    for h in range(heads):
        dots.append(est[:, 3 * h : 3 * h + 1] + est[:, 3 * h + 1 : 3 * h + 2] + est[:, 3 * h + 2 : 3 * h + 3])
    own_side = jnp.zeros((rows, 128), f32)
    for k, v in enumerate(dots):
        high = v.astype(bf16).astype(f32)
        own_side = jnp.where(lane == k, high, own_side)
        own_side = jnp.where(lane == len(dots) + k, v - high, own_side)
    ab = jnp.concatenate([sums[:rows, : 2 * adapt], own_side], axis=1).astype(bf16)
    rb[...] = mm(put_ref[...], ab).astype(bf16).reshape(rb.shape)

    row_ids = [new() for _ in range(shards)]
    for off in range(1, shards):
        to = shard_at(off)
        send(rb.at[to], rr.at[d], row_ids[off], {"section": s, "dp": to})
    rr[d] = rb[d]

    wo_ring.relay()
    wo_ring.finish()
    wo_ring.twins()
    gw_ring.start()

    wo_turned = wo_all[y, c].T
    for j in range(layers):
        rhs = jnp.where(j < s, gw_ref[...], wo_turned)
        tile = mm(wo_all[j // 2, j % 2], rhs).astype(bf16)
        tp[:, :, :, j * adapt : (j + 1) * adapt] = tile.reshape(SIDE, SIDE, shards, adapt)

    mid = layers * adapt // 2
    first = {}
    for off in (2, 1, 3):
        for n, axis in enumerate(("x", "z")):
            first[n, off] = new()
            to = step(axis, off)
            cut = pl.ds(n * mid, mid)
            src = tp.at[:, to, :, cut] if n == 0 else tp.at[to, :, :, cut]
            send(src, r1.at[n, off - 1], first[n, off], peer(axis, off))
    for off in range(1, shards):
        arrived(rr.at[shard_at(-off)], row_ids[off])
    tokens = mm(sel_ref[...], rr[...].reshape(shards * rr.shape[1], rr.shape[2]))
    own = tokens.shape[0] // layers
    for k in range(layers):
        sb[k, :own] = tokens[k * own : (k + 1) * own]
        sb[k, own : 2 * own, :] = jnp.zeros((own, sb.shape[2]), f32)
        for h in range(heads):
            line = sums[heads_by[h] : heads_by[h] + 3, adapt : 2 * adapt]
            sb[k, own + h : own + h + 1, :adapt] = jnp.sum(line, axis=0, keepdims=True)
    token_ids = [new() for _ in range(layers)]
    for off in range(1, layers):
        to = layer_at(off)
        send(sb.at[to], rq.at[s], token_ids[off], {"section": to, "dp": d})
    rq[s] = sb[s]
    second = {}
    for n in (0, 1):
        kept = tp[:, x, :, :mid] if n == 0 else tp[z, :, :, mid:]
        kept = kept.astype(f32)
        for off in (1, 3, 2):
            arrived(r1.at[n, off - 1], first[n, off])
            kept = kept + r1[n, off - 1].astype(f32)
        s1[n] = kept.astype(bf16)
        axis = ("z", "x")[n]
        for off in (2, 1, 3):
            second[n, off] = new()
            send(s1.at[n, step(axis, off)], r2.at[n, off - 1], second[n, off], peer(axis, off))
    gw_ring.relay()
    for n in (0, 1):
        kept = s1[n, me[("z", "x")[n]]].astype(f32)
        for off in (1, 3, 2):
            arrived(r2.at[n, off - 1], second[n, off])
            kept = kept + r2[n, off - 1].astype(f32)
        held[y, c, z, x, :, n * mid : (n + 1) * mid] = kept.astype(bf16)
    gather(lambda w, core, cut: held.at[w["y"], core, w["z"], w["x"], :, cut], layers * adapt)
    for off in range(1, layers):
        arrived(rq.at[layer_at(-off)], token_ids[off])
    for off in range(1, shards):
        src = x_all.at[c, shard_at(-off)]
        arrived(src, x_ids[off])
        send(src, src, x_swaps[off], twin)

    def tile(l, j):
        return held[l // 2, l % 2, :, :, :, j * adapt : (j + 1) * adapt].reshape(adapt, adapt)

    recurrence(layers, width, grad_scale, heads, tile, rq, side_ref, mine)
    swap = new()
    send(mine.at[1 - c], other, swap, twin)
    arrived(other, swap)
    a, b = mine[c], other[...]
    block[...] = jnp.concatenate([jnp.where(c == 0, a, b), jnp.where(c == 0, b, a)], axis=0).astype(
        bf16
    )
    pay[c, y, z, x] = block[...]

    def select():
        for off in range(1, shards):
            arrived(x_all.at[1 - c, shard_at(-off)], x_swaps[off])
        for copy in keep:
            copy.wait()
        quarter = x_sel.shape[0] // 4

        def batch(m, carried):
            start = pl.multiple_of(m * quarter, quarter)
            ids = lax.broadcasted_iota(jnp.int32, (quarter, place_ref.shape[1]), 0) + start
            seat = (ids == place_ref[...]).astype(f32).astype(bf16)
            for h in (0, 1):
                x_sel[pl.ds(start, quarter), h * wide : (h + 1) * wide] = mm(
                    seat, x_all[h].reshape(shards * rows, wide)
                ).astype(bf16)
            return carried

        lax.fori_loop(0, 4, batch, 0)

    gather(
        lambda w, core, cut: pay.at[core, w["y"], w["z"], w["x"], :, cut], block.shape[1], select
    )
    gw_ring.finish()
    gw_ring.twins()

    total = 2 * pay.shape[1] * shards * own

    def values(kind, at):
        cut = pl.ds(pl.multiple_of(at * adapt, adapt), adapt)
        return pay[kind, :, :, :, :, cut].reshape(total, adapt)

    def lanes(kind):
        return pay[kind, :, :, :, :, layers * adapt :].reshape(total, 128)

    act_t = values(0, s).T
    delta_t = values(1, s).T
    scal = lanes(0).astype(f32) + lanes(1).astype(f32)
    lane = lax.broadcasted_iota(jnp.int32, (total, 128), 1)
    sigma = jnp.sum(jnp.where(lane == s, scal, 0.0), axis=1, keepdims=True)
    head_sums = mm(act_t, lanes(0)) + mm(act_t, lanes(1))
    grad_out = -mm(act_t, (x_sel[...].astype(f32) * sigma).astype(bf16))
    for h in range(heads):
        grad_out += head_sums[:, layers + h : layers + h + 1] * head_ref[h : h + 1, :]
    grad_out_ref[...] = grad_out
    turned = sums_t
    turned[...] = mm(delta_t, x_sel[...])

    def layer(j, carried):
        jy, jc = j // 2, j % 2
        by = jnp.sum(jnp.where(lane == jnp.maximum(j, s), scal, 0.0), axis=1, keepdims=True)
        acts = values(0, j)
        scaled = (acts.astype(f32) * -by).astype(bf16)
        grad_out_ref[...] += mm(mm(act_t, scaled).astype(bf16), wo_all[jy, jc])

        @pl.when(j > s)
        def _():
            grad_out_ref[...] += mm(mm(act_t, values(1, j)).astype(bf16), gw_all[jy, jc], NT)

        @pl.when(j < s)
        def _():
            turned[...] += mm(mm(delta_t, acts).astype(bf16), wo_all[jy, jc])

        return carried

    lax.fori_loop(0, layers, layer, 0)
    grad_in_ref[...] = (turned[...] * scale_ref[...]).T
    loss = jnp.sum(jnp.where(lane == layers + heads, scal, 0.0), axis=0, keepdims=True)
    loss_ref[...] = jnp.broadcast_to(jnp.sum(loss, axis=1, keepdims=True) / total, loss_ref.shape)
    for copy in issued:
        copy.wait_send()


def recurrence(layers, width, grad_scale, heads, tile, rows_ref, side_ref, out_ref):
    adapt = 256
    own = side_ref.shape[0]
    sums = rows_ref[0, :own, 2 * adapt :]
    side = side_ref[...]
    part = lambda k: sums[:, k : k + 1] + sums[:, 1 + heads + k : 2 + heads + k]
    sq = part(0)
    est = [part(1 + k) for k in range(heads)]
    mask = side[:, 0:1]
    target = [side[:, 1 + k : 2 + k] for k in range(heads)]
    coef = [side[:, 4 + k : 5 + k] for k in range(heads)]
    into = [rows_ref[k, :own, :adapt] for k in range(layers)]
    onto = [rows_ref[k, :own, adapt : 2 * adapt] for k in range(layers)]
    head_out = [
        [rows_ref[k, own + h : own + h + 1, :adapt] for h in range(heads)] for k in range(layers)
    ]
    pre, fac, kept = [], [], {}
    for j in range(layers):
        f = lax.rsqrt(jnp.maximum(sq, 0.0) / width + EPS)
        p = f * into[j]
        act = (p * jax.nn.sigmoid(p)).astype(bf16)
        wide = act.astype(f32)
        out_ref[0, :, j * adapt : (j + 1) * adapt] = wide
        pre.append(p)
        fac.append(f)
        for k in range(j):
            kept[j, k] = onto[k]
        before = onto[j]
        for k in range(layers):
            if k <= j:
                onto[k] = onto[k] + mm(act, tile(k, j))
            else:
                into[k] = into[k] + mm(act, tile(k, j))
                onto[k] = onto[k] + mm(act, tile(j, k), NT)
        sq = sq + jnp.sum(wide * (before + onto[j]), axis=1, keepdims=True)
        for h in range(heads):
            est[h] = est[h] + jnp.sum(wide * head_out[j][h], axis=1, keepdims=True)
    f = lax.rsqrt(jnp.maximum(sq, 0.0) / width + EPS)
    loss = jnp.zeros_like(sq)
    along = jnp.zeros_like(sq)
    lane = lax.broadcasted_iota(jnp.int32, (own, 128), 1)
    extra = jnp.zeros(lane.shape, f32)
    grads = []
    for h in range(heads):
        e = f * est[h]
        err = e - target[h]
        weighted = coef[h] * mask * err
        loss = loss + 0.5 * weighted * err
        scaled = weighted * grad_scale
        along = along + scaled * e
        grads.append(f * scaled)
        extra = jnp.where(lane == layers + h, grads[h], extra)
    extra = jnp.where(lane == layers + heads, loss, extra)
    total = f * f * along / width
    back = []
    for k in range(layers):
        start = -total * onto[k]
        for h in range(heads):
            start = start + grads[h] * head_out[k][h]
        back.append(start)
    for l in range(layers - 1, -1, -1):
        extra = jnp.where(lane == l, total, extra)
        sg = jax.nn.sigmoid(pre[l])
        delta = (fac[l] * (back[l] * sg * (1.0 + pre[l] * (1.0 - sg)))).astype(bf16)
        wide = delta.astype(f32)
        out_ref[1, :, l * adapt : (l + 1) * adapt] = wide
        s = fac[l] / width * jnp.sum(wide * pre[l], axis=1, keepdims=True)
        total = total + s
        for k in range(l):
            back[k] = back[k] + mm(delta, tile(l, k), NT) - s * kept[l, k]
    high = extra.astype(bf16).astype(f32)
    out_ref[0, :, layers * adapt :] = high
    out_ref[1, :, layers * adapt :] = extra - high


def local(
    hidden,
    lengths,
    response_mask,
    norm_gain,
    weight_in,
    weight_out,
    final_gain,
    value_heads,
    old_values,
    advantages,
    multipliers,
):
    shards = lax.axis_size("dp")
    layers = lax.axis_size("section")
    d = lax.axis_index("dp")
    l = lax.axis_index("section")
    micro, cap, width = hidden.shape
    heads = value_heads.shape[0]
    adapt = weight_in.shape[2]
    total = micro * BAL * shards
    part = width // shards
    own = total // (shards * layers)
    per_micro = total // micro

    gain = norm_gain[0]
    scale_sl = lax.dynamic_slice(gain, (d * part,), (part,))
    gw_sl = lax.dynamic_slice(weight_in[0], (d * part, 0), (part, adapt))
    gw_sl = (scale_sl[:, None] * gw_sl.astype(f32)).astype(bf16)

    gfh = final_gain * value_heads
    head_sl = lax.dynamic_slice(gfh, (0, d * part), (heads, part))
    head_sl = jnp.concatenate([head_sl, jnp.zeros((8 - heads, part), f32)], axis=0)
    terms = jnp.stack(split(gfh, 3), axis=1).reshape(3 * heads, width)
    x0 = jnp.concatenate(
        [
            hidden.reshape(micro * cap, width),
            terms,
            jnp.zeros((128 - 3 * heads, width), bf16),
        ],
        axis=0,
    )
    ends = jnp.cumsum(lengths, axis=1)
    begins = ends - lengths
    offsets = jnp.arange(cap, dtype=jnp.int32)
    batches = jnp.arange(micro, dtype=jnp.int32)
    most = 3
    begin = jnp.take(begins, d, axis=1)[:, None]
    p = begin + offsets[None]
    n = p // shards - (begin - p % shards + shards - 1) // shards
    slot = (p % shards) * 16 + batches[:, None] * most + n
    slot = jnp.where(offsets[None] < jnp.take(lengths, d, axis=1)[:, None], slot, -1).reshape(-1)
    put = (jnp.arange(shards * 16, dtype=jnp.int32)[:, None] == slot[None]).astype(bf16)
    q = (begins - d + shards - 1) // shards
    p = d + shards * (q[:, :, None] + jnp.arange(most, dtype=jnp.int32))
    seat = (2 * batches[:, None, None] + p // 128) * own + (p // shards) % own
    seat = jnp.where(p < ends[:, :, None], seat, -1)
    seat = jnp.swapaxes(seat, 0, 1).reshape(shards, micro * most)
    seat = jnp.pad(seat, ((0, 0), (0, 16 - micro * most)), constant_values=-1).reshape(-1)
    sel = (jnp.arange(layers * own, dtype=jnp.int32)[:, None] == seat[None]).astype(bf16)

    token = jnp.where(
        offsets[None, None, :] < lengths[:, :, None],
        begins[:, :, None] + offsets[None, None, :],
        -1,
    )
    batch = l // 2
    ids = (l % 2) * 128 + shards * jnp.arange(own, dtype=jnp.int32) + d
    spot = lax.dynamic_index_in_dim(token, batch, 0, keepdims=False).reshape(-1)
    pick = (ids[:, None] == spot[None, :]).astype(f32)
    used = lax.dynamic_index_in_dim(response_mask, batch, 0, keepdims=False).astype(f32)
    aims = lax.dynamic_index_in_dim(old_values + advantages, batch, 1, keepdims=False)
    mask = jnp.sum(pick * used[None, :], axis=1, keepdims=True)
    aim = jnp.sum(pick[:, None, :] * aims[None], axis=2)
    coef = jnp.concatenate([jnp.ones((1,), f32), multipliers])
    side = jnp.concatenate(
        [
            mask,
            aim,
            jnp.broadcast_to(coef[None], (own, heads)),
            jnp.zeros((own, 127 - 2 * heads), f32),
        ],
        axis=1,
    )

    place = (batches[:, None, None] * shards + token % shards) * 16 + token // 128 * own
    place = jnp.where(token >= 0, place + token // shards % own, -1)
    place = jnp.swapaxes(place, 0, 1).reshape(1, -1)

    vm = pl.BlockSpec(memory_space=pltpu.VMEM)
    hbm = pl.BlockSpec(memory_space=pl.ANY)
    columns = layers * adapt + 128
    wide = 2 * adapt + 128
    half = layers * adapt // 2
    grad_in, grad_out, loss = pl.pallas_call(
        functools.partial(kernel, layers, float(width), LOSS_SCALE / total),
        out_shape=(
            jax.ShapeDtypeStruct((part, adapt), f32),
            jax.ShapeDtypeStruct((adapt, part), f32),
            jax.ShapeDtypeStruct((8, 128), f32),
        ),
        in_specs=[hbm, hbm] + [vm] * 9,
        out_specs=(vm, vm, vm),
        scratch_shapes=[
            pltpu.VMEM((shards, part, adapt), bf16),
            pltpu.VMEM((shards, adapt, part), bf16),
            pltpu.VMEM((x0.shape[0], wide), f32),
            pltpu.VMEM((SIDE, 2, adapt, part), bf16),
            pltpu.VMEM((SIDE, 2, part, adapt), bf16),
            pltpu.VMEM((2, shards, micro * cap, part // 2), bf16),
            pltpu.VMEM((total, part), bf16),
            pltpu.VMEM((2, SIDE, SIDE, SIDE, 16, columns), bf16),
            pltpu.VMEM((shards, 16, wide), bf16),
            pltpu.VMEM((SIDE, SIDE, 16, layers * adapt), bf16),
            pltpu.VMEM((2, 3, SIDE, 16, half), bf16),
            pltpu.VMEM((2, SIDE, 16, half), bf16),
            pltpu.VMEM((2, 3, 16, half), bf16),
            pltpu.VMEM((SIDE, 2, SIDE, SIDE, 16, layers * adapt), bf16),
            pltpu.VMEM((shards, 16, wide), bf16),
            pltpu.VMEM((layers, 2 * own, wide), f32),
            pltpu.VMEM((layers, 2 * own, wide), f32),
            pltpu.VMEM((2, own, columns), f32),
            pltpu.VMEM((own, columns), f32),
            pltpu.VMEM((16, columns), bf16),
            pltpu.VMEM((adapt, part), f32),
            pltpu.SemaphoreType.DMA((COPIES,)),
            pltpu.SemaphoreType.DMA((COPIES,)),
            pltpu.SemaphoreType.DMA((40,)),
        ],
        compiler_params=pltpu.CompilerParams(
            vmem_limit_bytes=60 * 1024 * 1024, collective_id=0, has_side_effects=True
        ),
        cost_estimate=pl.CostEstimate(
            flops=10**10, bytes_accessed=3 * 10**7, transcendentals=0
        ),
        name="layers",
    )(
        weight_in[0],
        weight_out[0],
        gw_sl,
        gain[None],
        x0,
        put,
        sel,
        side,
        place,
        head_sl,
        scale_sl[None],
    )
    return (grad_in[None], grad_out[None], loss[0, 0])


def solution(mesh):
    return jax.shard_map(
        local,
        mesh=mesh,
        in_specs=(
            P(None, "dp", None),
            P(),
            P(),
            P("section", None),
            P("section", None, None),
            P("section", None, None),
            P(),
            P(),
            P(),
            P(),
            P(),
        ),
        out_specs=(P("section", "dp", None), P("section", None, "dp"), P()),
        check_vma=False,
    )
```

profile of v0, /device:TPU:1, one launch (start us, length us, event | category | flops | bytes accessed | tf_op | source)
XLA Modules:
  0.0 154.3 jit_solution(2212892686353680915)
XLA Ops:
  0.6 0.7 constant_dynamic-slice_fusion.5.scale_ref
  1.3 1.8 %fusion.gw_ref = bf16[512,256]{1,0:T(8,128)(2,1)} fusion(bf16[1,8192,256]{2,1,0:T(8,128)(2,1)} %param.17, s32[]{:T(128)S(6)} %select_n.175, f32[512]{0:T(512)S(1)} %bitcast.35), kind=kLoop, calls=%fused_computation.2 | loop fusion | flops 393216 | bytes 526340 | tf_op jit(solution)/shard_map/convert_element_type | solution.py:560
  3.1 1.0 convert_bitcast_fusion
  4.1 0.2 pad_maximum_fusion
  4.3 0.2 copy.32
  4.5 0.1 reshape.379
  4.6 3.0 %copy.31 = bf16[4,36,8192]{2,1,0:T(8,128)(2,1)S(1)} copy(bf16[4,36,8192]{2,0,1:T(4,128)(2,1)} %param.13) | data formatting | bytes 4718592 | tf_op args[0]
  7.6 1.8 %reshape.378 = bf16[144,8192]{1,0:T(8,128)(2,1)} reshape(bf16[4,36,8192]{2,1,0:T(8,128)(2,1)S(1)} %copy.31) | data formatting | bytes 4718592 | tf_op jit(solution)/shard_map/reshape | solution.py:568
  9.4 4.4 %maximum_maximum_fusion.x0_ref = bf16[272,8192]{1,0:T(8,128)(2,1)} fusion(bf16[9,8192]{1,0:T(8,128)(2,1)S(1)} %reshape.379, bf16[144,8192]{1,0:T(8,128)(2,1)} %reshape.378, bf16[272]{0:T(512)(128)(2,1)S(1)} %pad.16.clone), kind=kLoop, calls=%fused_computation | loop fusion | flops 13369344 | bytes 6963744 | tf_op jit(solution)/shard_map/concatenate | solution.py:566
  13.9 0.2 reduce_window_sum.11
  14.1 0.2 fusion.21
  14.8 0.7 fusion.1.put_ref
  16.1 0.6 fusion.5.sel_ref
  16.7 0.8 dynamic-slice_add_fusion
  18.0 0.7 convert_reduce_fusion
  18.7 0.2 fusion.6
  19.1 0.7 maximum_maximum_fusion.1.side_ref
  20.3 0.1 add.334
  20.4 0.7 compare_select_fusion.2.place_ref
  21.1 0.6 concatenate.15.head_ref
  21.7 127.6 %layers.1 = (f32[512,256]{1,0:T(8,128)}, f32[256,512]{1,0:T(8,128)}, f32[8,128]{1,0:T(8,128)}) custom-call(bf16[8192,256]{1,0:T(8,128)(2,1)} %bitcast.34, bf16[256,8192]{1,0:T(8,128)(2,1)} %bitcast.37, bf16[512,256]{1,0:T(8,128)(2,1)} %fusion.gw_ref, f32[1,8192]{1,0:T(1,128)} %gain_ref.1, bf16[272,8192]{1,0:T(8,128)(2,1)} %maximum_maximum_fusion.x0_ref, ...), custom_call_target="tpu_custom_call" | custom-call | flops 10000000000 | bytes 30000000 | tf_op jit(solution)/shard_map/layers/pallas_call | solution.py:626
  149.4 1.2 slice.3
  150.6 1.9 %copy.44 = f32[1,512,256]{2,1,0:T(8,128)} copy(f32[1,512,256]{2,1,0:T(8,128)} %bitcast.29) | data formatting | bytes 1048576
  152.4 1.9 %copy.45 = f32[1,256,512]{2,1,0:T(8,128)} copy(f32[1,256,512]{2,1,0:T(8,128)} %bitcast.28) | data formatting | bytes 1048576
  (52 shorter events, 2.4 us)
Async XLA Ops:
  1.3 8.0 %copy-start.1 = (f32[1,512]{1,0:T(1,128)}, f32[1,512]{1,0:T(1,128)S(1)}, u32[]{:S(2)}) copy-start(f32[1,512]{1,0:T(1,128)S(1)} %constant_dynamic-slice_fusion.5.scale_ref) | copy-start | bytes 6148
  9.3 4.6 %copy-start = (s32[4,16]{1,0:T(4,128)S(1)}, s32[4,16]{1,0:T(4,128)}, u32[]{:S(2)}) copy-start(s32[4,16]{1,0:T(4,128)} %param.14) | copy-start | bytes 772
  9.4 9.7 %copy-start.2 = (f32[2]{0:T(128)S(1)}, f32[2]{0:T(128)}, u32[]{:S(2)}) copy-start(f32[2]{0:T(128)} %param.23) | copy-start | bytes 28
where the time goes:
time: 155 us; the launch traced here: 154 us
  Pallas kernels  128 us (83%)
  local copies, waits for them, and re-layouts  13.2 us (9%)
  other arithmetic  12.7 us (8%)
    pallas_call x1, Pallas kernels, local(): pl.pallas_call(functools.partial(kernel, layers, float(width), LOSS_SCALE...  128 us
    unnamed x11, local copies, waits for them, and re-layouts  6.82 us
    concatenate x1, other arithmetic, local(): jnp.concatenate([hidden.reshape(micro * cap, width), terms, jnp.zeros((12...  4.38 us

commit v1 on v0

--- a/solution.py
+++ b/solution.py
@@ -18,48 +18,39 @@
 NN = (((1,), (0,)), ((), ()))
 MESH = pl.DeviceIdType.MESH
 SIDE = 4
-COPIES = 288
+COPIES = 360
 
 
 def mm(a, b, dims=NN):
     return lax.dot_general(a, b, dims, preferred_element_type=f32)
 
-
-def exact(a, b, dims):
-    return lax.dot_general(
-        a, b, dims, precision=lax.Precision.HIGHEST, preferred_element_type=f32
-    )
-
-
-def split(v, terms):
-    out = []
-    for _ in range(terms):
-        hi = v.astype(bf16)
-        out.append(hi)
-        v = v - hi.astype(f32)
-    return out
 
 def kernel(
     layers,
     width,
     grad_scale,
+    lengths_ref,
+    coef_ref,
     win_ref,
     wout_ref,
-    gw_ref,
     gain_ref,
-    x0_ref,
-    put_ref,
-    sel_ref,
-    side_ref,
-    place_ref,
+    hid_ref,
+    final_ref,
     head_ref,
-    scale_ref,
+    mask_ref,
+    old_ref,
+    adv_ref,
     grad_in_ref,
     grad_out_ref,
     loss_ref,
     win,
     wout,
     sums,
+    est,
+    xf,
+    terms,
+    tokens_at,
+    xm,
     wo_all,
     gw_all,
     x_all,
@@ -88,9 +79,10 @@
     z, x = d // SIDE, d % SIDE
     me = {"x": x, "y": y, "z": z}
     shards = SIDE * SIDE
-    part, adapt = gw_ref.shape
-    heads = 3
-    rows = put_ref.shape[1]
+    chunks, part, adapt = win.shape
+    heads = head_ref.shape[0]
+    micro, cap = hid_ref.shape[:2]
+    rows = micro * cap
     step = lambda a, off: (me[a] + off + SIDE) % SIDE
 
     def peer(axis, off):
@@ -204,31 +196,79 @@
         third = (columns // 384) * 128
         bounds = [0, third, 2 * third, columns]
         orders = [("x", "z", "y"), ("z", "y", "x"), ("y", "x", "z")]
-        for phase in range(3):
-            rings = []
-            for p, order in enumerate(orders):
-                lo, hi = bounds[p], bounds[p + 1]
-                mid = lo + ((hi - lo) // 256) * 128
-                cuts = [(lo, mid - lo), (mid, hi - mid)]
-
-                def slab(v, h, core, order=order, cuts=cuts):
-                    where = dict(me)
-                    for a in order[:phase]:
-                        where[a] = pl.ds(0, SIDE)
-                    where[order[phase]] = step(order[phase], v)
-                    return at(where, core, pl.ds(*cuts[h]))
-
-                rings.append(Ring(order[phase], slab, swaps=phase == 2))
-            for ring in rings:
-                ring.start()
-            if phase == 2 and meanwhile is not None:
-                meanwhile()
-            for ring in rings:
-                ring.relay()
-            for ring in rings:
-                ring.finish()
-        for ring in rings:
-            ring.twins()
+        parts = range(3)
+
+        def ref(p, core, *steps):
+            where = {
+                axis: pl.ds(0, SIDE) if v is None else step(axis, v)
+                for axis, v in zip(orders[p], steps)
+            }
+            return at(where, core, pl.ds(bounds[p], bounds[p + 1] - bounds[p]))
+
+        ids, swaps = {}, {}
+
+        def put(at_, block, to):
+            ids[at_] = new()
+            send(block, block, ids[at_], to)
+
+        def swap(p, row, v):
+            swaps[p, row, v] = new()
+            block = ref(p, c, None, row, v)
+            send(block, block, swaps[p, row, v], twin)
+
+        def ring(p, row):
+            axis = orders[p][2]
+            for off in (1, -1):
+                put((p, row, off), ref(p, c, None, row, 0), peer(axis, off))
+            swap(p, row, 0)
+
+        way = {0: 1, -1: -1, -3: 1, -2: -1}
+
+        def relay(p, row):
+            g = way[row]
+            block = ref(p, c, None, row, -g)
+            arrived(block, ids[p, row, g])
+            put((p, row, 2), block, peer(orders[p][2], g))
+            swap(p, row, -g)
+
+        def end(p, row, v, n):
+            arrived(ref(p, c, None, row, v), ids[p, row, n])
+            swap(p, row, v)
+
+        for off in (2, 1, 3):
+            for p in parts:
+                put((0, p, off, "a"), ref(p, c, 0, 0, 0), peer(orders[p][0], off))
+        for off in (1, 3, 2):
+            for p in parts:
+                arrived(ref(p, c, -off, 0, 0), ids[0, p, off, "a"])
+        for off in (2, 1, 3):
+            for p in parts:
+                put((1, p, off, "b"), ref(p, c, None, 0, 0), peer(orders[p][1], off))
+        for p in parts:
+            ring(p, 0)
+        for off in (1, 3):
+            for p in parts:
+                arrived(ref(p, c, None, -off, 0), ids[1, p, off, "b"])
+                ring(p, -off)
+        for p in parts:
+            relay(p, 0)
+        for p in parts:
+            arrived(ref(p, c, None, -2, 0), ids[1, p, 2, "b"])
+            ring(p, -2)
+        if meanwhile is not None:
+            meanwhile()
+        order = (0, -1, -3, -2)
+        for row in order[1:]:
+            for p in parts:
+                relay(p, row)
+        for row in order:
+            for p in parts:
+                end(p, row, way[row], -way[row])
+        for row in order:
+            for p in parts:
+                end(p, row, 2, 2)
+        for (p, row, v), at_ in swaps.items():
+            arrived(ref(p, 1 - c, None, row, v), at_)
 
     chunks = win.shape[0]
     loads = []
@@ -248,7 +288,7 @@
     for h in (0, 1):
         keep.append(
             local(
-                x0_ref.at[:rows, pl.ds(pl.multiple_of(d * part + h * wide, wide), wide)],
+                hid_ref.at[:, :, pl.ds(pl.multiple_of(d * part + h * wide, wide), wide)],
                 x_all.at[h, d],
             )
         )
@@ -257,49 +297,122 @@
     for off in range(1, shards):
         to = shard_at(off)
         send(
-            x0_ref.at[:rows, pl.ds(pl.multiple_of(to * part + c * wide, wide), wide)],
+            hid_ref.at[:, :, pl.ds(pl.multiple_of(to * part + c * wide, wide), wide)],
             x_all.at[c, d],
             x_ids[off],
             {"section": s, "dp": to},
         )
-    long = part // 2
     gw_ring = Ring(
-        "y", lambda v, h, core: gw_all.at[step("y", v), core, pl.ds(h * long, long)], True
+        "y", lambda v, h, core: gw_all.at[step("y", v), core, pl.ds(h * half, half)], True
     )
-    gw_all[y, c] = gw_ref[...]
+
+    begin = [[None] * shards for _ in range(micro)]
+    length = [[lengths_ref[m, i] for i in range(shards)] for m in range(micro)]
+    mine_at = []
+    for m in range(micro):
+        at, here = jnp.int32(0), jnp.int32(0)
+        for i in range(shards):
+            begin[m][i] = at
+            here = here + jnp.where(i < d, length[m][i], 0)
+            at = at + length[m][i]
+        mine_at.append(here)
+    lane = lax.broadcasted_iota(jnp.int32, (1, rows), 1)
+    m_of, b_of, n_of = jnp.zeros_like(lane), jnp.zeros_like(lane), jnp.zeros_like(lane)
+    for m in range(micro):
+        m_of = jnp.where(lane >= m * cap, m, m_of)
+        b_of = jnp.where(lane >= m * cap, mine_at[m], b_of)
+        n_of = jnp.where(lane >= m * cap, lengths_ref[m, d], n_of)
+    r_of = lane - m_of * cap
+    p = b_of + r_of
+    n = (p >> 4) - ((b_of - (p & 15) + 15) >> 4)
+    slot = jnp.where(r_of < n_of, (p & 15) * 16 + m_of * 3 + n, -1)
+    put_rows = lax.broadcasted_iota(jnp.int32, (shards * 16, rows), 0) == slot
+    put_rows = jnp.where(put_rows, 1.0, 0.0).astype(bf16)
+    lane = lax.broadcasted_iota(jnp.int32, (1, shards * 16), 1)
+    src, n = lane >> 4, lane & 15
+    m_of = jnp.where(n >= 3, 1, 0) + jnp.where(n >= 6, 1, 0) + jnp.where(n >= 9, 1, 0)
+    b_of, n_of = jnp.zeros_like(lane), jnp.zeros_like(lane)
+    for m in range(micro):
+        b, e = jnp.zeros_like(lane), jnp.zeros_like(lane)
+        for i in range(shards):
+            b = jnp.where(src == i, begin[m][i], b)
+            e = jnp.where(src == i, begin[m][i] + length[m][i], e)
+        b_of = jnp.where(m_of == m, b, b_of)
+        n_of = jnp.where(m_of == m, e, n_of)
+    p = d + 16 * (((b_of - d + 15) >> 4) + n - 3 * m_of)
+    seat = (2 * m_of + (p >> 7)) * 8 + ((p >> 4) & 7)
+    seat = jnp.where(p < n_of, jnp.where(n < 12, seat, -1), -1)
+    take_rows = lax.broadcasted_iota(jnp.int32, (layers * 8, shards * 16), 0) == seat
+    take_rows = jnp.where(take_rows, 1.0, 0.0).astype(bf16)
+    lane = lax.broadcasted_iota(jnp.int32, (1, shards * cap), 1)
+    ids = lax.broadcasted_iota(jnp.int32, (8, shards * cap), 0) * 16 + (s % 2) * 128 + d
+    batch = s // 2
+    spot = jnp.zeros_like(lane)
+    used = jnp.zeros(lane.shape, f32)
+    aims = [jnp.zeros(lane.shape, f32) for _ in range(heads)]
+    for m in range(micro):
+        b, e, first_lane = jnp.zeros_like(lane), jnp.zeros_like(lane), jnp.zeros_like(lane)
+        for i in range(shards):
+            b = jnp.where(lane >= i * cap, begin[m][i], b)
+            e = jnp.where(lane >= i * cap, length[m][i], e)
+            first_lane = jnp.where(lane >= i * cap, i * cap, first_lane)
+        row = lane - first_lane
+        row = jnp.where(row < e, b + row, -1)
+        tokens_at[m] = row
+        spot = jnp.where(batch == m, row, spot)
+        used = jnp.where(batch == m, mask_ref[m : m + 1, :].astype(f32), used)
+        for h in range(heads):
+            aim = old_ref[h, m : m + 1, :] + adv_ref[h, m : m + 1, :]
+            aims[h] = jnp.where(batch == m, aim, aims[h])
+    pick = ids == spot
+    mask = jnp.sum(jnp.where(pick, used, 0.0), axis=1, keepdims=True)
+    target = [jnp.sum(jnp.where(pick, aim, 0.0), axis=1, keepdims=True) for aim in aims]
 
     square = jnp.zeros((rows, 128), f32)
+    sums[...] = jnp.zeros(sums.shape, f32)
+    est[...] = jnp.zeros(est.shape, f32)
+    terms[...] = jnp.zeros(terms.shape, f32)
     for copy in loads:
         copy.wait()
-    sums[...] = jnp.zeros(sums.shape, f32)
 
     def chunk(k, square):
         cut = pl.ds(pl.multiple_of(k * part, part), part)
-        both = x0_ref[:, cut]
-        x = both[:rows].astype(f32)
+        for m in range(micro):
+            xf[m * cap : (m + 1) * cap, :] = hid_ref[m, :, cut].astype(f32)
+        left = final_ref[:, cut] * head_ref[:, cut]
+        for t in range(3):
+            term = left.astype(bf16).astype(f32)
+            terms[8 * t : 8 * t + heads, :] = term
+            left = left - term
+        x = xf[...]
         for i in range(part // 128):
             piece = x[:, i * 128 : (i + 1) * 128]
             square = square + piece * piece
-        gained = (x * gain_ref[:, cut]).astype(bf16)
-        sums[:rows, :adapt] += mm(gained, win[k])
+        lines = terms[...].astype(bf16)
+        x16 = x.astype(bf16)
+        both = jnp.concatenate([x16, lines], axis=0)
+        sums[:rows, :adapt] += mm((x * gain_ref[:, cut]).astype(bf16), win[k])
         sums[:, adapt : 2 * adapt] += mm(both, wout[k], NT)
-        sums[:rows, 2 * adapt :] += mm(both[:rows], both[rows:], NT)
+        est[...] += mm(x16, lines, NT)
         return square
 
-    square = jnp.sum(lax.fori_loop(0, chunks, chunk, square), axis=1, keepdims=True)
-    heads_by = [rows + 3 * h for h in range(heads)]
-    est = sums[:rows, 2 * adapt :]
+    square = lax.fori_loop(0, chunks // 2, chunk, square)
+    wo_ring.relay()
+    square = lax.fori_loop(chunks // 2, chunks, chunk, square)
+    square = jnp.sum(square, axis=1, keepdims=True)
+    gw_own = (win[d].astype(f32).T * gain_ref[:, columns]).astype(bf16)
+    gw_all[y, c] = gw_own
     lane = lax.broadcasted_iota(jnp.int32, (rows, 128), 1)
     dots = [square]
     for h in range(heads):
-        dots.append(est[:, 3 * h : 3 * h + 1] + est[:, 3 * h + 1 : 3 * h + 2] + est[:, 3 * h + 2 : 3 * h + 3])
+        dots.append(est[:, h : h + 1] + est[:, 8 + h : 9 + h] + est[:, 16 + h : 17 + h])
     own_side = jnp.zeros((rows, 128), f32)
     for k, v in enumerate(dots):
         high = v.astype(bf16).astype(f32)
         own_side = jnp.where(lane == k, high, own_side)
         own_side = jnp.where(lane == len(dots) + k, v - high, own_side)
-    ab = jnp.concatenate([sums[:rows, : 2 * adapt], own_side], axis=1).astype(bf16)
-    rb[...] = mm(put_ref[...], ab).astype(bf16).reshape(rb.shape)
+    ab = jnp.concatenate([sums[:rows, :], own_side], axis=1).astype(bf16)
+    rb[...] = mm(put_rows, ab).astype(bf16).reshape(rb.shape)
 
     row_ids = [new() for _ in range(shards)]
     for off in range(1, shards):
@@ -307,15 +420,14 @@
         send(rb.at[to], rr.at[d], row_ids[off], {"section": s, "dp": to})
     rr[d] = rb[d]
 
-    wo_ring.relay()
     wo_ring.finish()
     wo_ring.twins()
     gw_ring.start()
 
-    wo_turned = wo_all[y, c].T
+    wo_own = wo_all[y, c]
     for j in range(layers):
-        rhs = jnp.where(j < s, gw_ref[...], wo_turned)
-        tile = mm(wo_all[j // 2, j % 2], rhs).astype(bf16)
+        rhs = jnp.where(j < s, gw_own, wo_own)
+        tile = mm(wo_all[j // 2, j % 2], rhs, NT).astype(bf16)
         tp[:, :, :, j * adapt : (j + 1) * adapt] = tile.reshape(SIDE, SIDE, shards, adapt)
 
     mid = layers * adapt // 2
@@ -329,14 +441,17 @@
             send(src, r1.at[n, off - 1], first[n, off], peer(axis, off))
     for off in range(1, shards):
         arrived(rr.at[shard_at(-off)], row_ids[off])
-    tokens = mm(sel_ref[...], rr[...].reshape(shards * rr.shape[1], rr.shape[2]))
+    tokens = mm(take_rows, rr[...].reshape(shards * rr.shape[1], rr.shape[2]))
     own = tokens.shape[0] // layers
+    lines = []
+    for h in range(heads):
+        at = rows + h
+        lines.append(sum(sums[at + 8 * t : at + 8 * t + 1, adapt:] for t in range(3)))
     for k in range(layers):
         sb[k, :own] = tokens[k * own : (k + 1) * own]
         sb[k, own : 2 * own, :] = jnp.zeros((own, sb.shape[2]), f32)
         for h in range(heads):
-            line = sums[heads_by[h] : heads_by[h] + 3, adapt : 2 * adapt]
-            sb[k, own + h : own + h + 1, :adapt] = jnp.sum(line, axis=0, keepdims=True)
+            sb[k, own + h : own + h + 1, :adapt] = lines[h]
     token_ids = [new() for _ in range(layers)]
     for off in range(1, layers):
         to = layer_at(off)
@@ -355,6 +470,10 @@
             second[n, off] = new()
             send(s1.at[n, step(axis, off)], r2.at[n, off - 1], second[n, off], peer(axis, off))
     gw_ring.relay()
+    for off in range(1, shards):
+        src = x_all.at[c, shard_at(-off)]
+        arrived(src, x_ids[off])
+        send(src, src, x_swaps[off], twin)
     for n in (0, 1):
         kept = s1[n, me[("z", "x")[n]]].astype(f32)
         for off in (1, 3, 2):
@@ -364,15 +483,12 @@
     gather(lambda w, core, cut: held.at[w["y"], core, w["z"], w["x"], :, cut], layers * adapt)
     for off in range(1, layers):
         arrived(rq.at[layer_at(-off)], token_ids[off])
-    for off in range(1, shards):
-        src = x_all.at[c, shard_at(-off)]
-        arrived(src, x_ids[off])
-        send(src, src, x_swaps[off], twin)
 
     def tile(l, j):
         return held[l // 2, l % 2, :, :, :, j * adapt : (j + 1) * adapt].reshape(adapt, adapt)
 
-    recurrence(layers, width, grad_scale, heads, tile, rq, side_ref, mine)
+    coef = [1.0, coef_ref[0], coef_ref[1]]
+    recurrence(layers, width, grad_scale, tile, rq, mask, target, coef, mine)
     swap = new()
     send(mine.at[1 - c], other, swap, twin)
     arrived(other, swap)
@@ -387,19 +503,20 @@
             arrived(x_all.at[1 - c, shard_at(-off)], x_swaps[off])
         for copy in keep:
             copy.wait()
-        quarter = x_sel.shape[0] // 4
-
-        def batch(m, carried):
+        quarter = x_sel.shape[1] // micro
+        at = lax.broadcasted_iota(jnp.int32, (quarter, shards * cap), 0)
+        token = ((at >> 3) & 1) * 128 + (at & 7) * 16 + (at >> 4)
+
+        def batch(i, carried):
+            m, h = i // 2, i % 2
+            for src in range(shards):
+                xm[src * cap : (src + 1) * cap, :] = x_all[h, src, m].astype(f32)
+            seat = jnp.where(token == tokens_at[m], 1.0, 0.0).astype(bf16)
             start = pl.multiple_of(m * quarter, quarter)
-            ids = lax.broadcasted_iota(jnp.int32, (quarter, place_ref.shape[1]), 0) + start
-            seat = (ids == place_ref[...]).astype(f32).astype(bf16)
-            for h in (0, 1):
-                x_sel[pl.ds(start, quarter), h * wide : (h + 1) * wide] = mm(
-                    seat, x_all[h].reshape(shards * rows, wide)
-                ).astype(bf16)
+            x_sel[h, pl.ds(start, quarter), :] = mm(seat, xm[...].astype(bf16)).astype(bf16)
             return carried
 
-        lax.fori_loop(0, 4, batch, 0)
+        lax.fori_loop(0, 2 * micro, batch, 0)
 
     gather(
         lambda w, core, cut: pay.at[core, w["y"], w["z"], w["x"], :, cut], block.shape[1], select
@@ -422,12 +539,14 @@
     lane = lax.broadcasted_iota(jnp.int32, (total, 128), 1)
     sigma = jnp.sum(jnp.where(lane == s, scal, 0.0), axis=1, keepdims=True)
     head_sums = mm(act_t, lanes(0)) + mm(act_t, lanes(1))
-    grad_out = -mm(act_t, (x_sel[...].astype(f32) * sigma).astype(bf16))
+    turned = sums_t
+    for n in (0, 1):
+        cut = slice(n * wide, (n + 1) * wide)
+        grad_out_ref[:, cut] = -mm(act_t, (x_sel[n].astype(f32) * sigma).astype(bf16))
+        turned[:, cut] = mm(delta_t, x_sel[n])
+    gfh = final_ref[:, columns] * head_ref[:, columns]
     for h in range(heads):
-        grad_out += head_sums[:, layers + h : layers + h + 1] * head_ref[h : h + 1, :]
-    grad_out_ref[...] = grad_out
-    turned = sums_t
-    turned[...] = mm(delta_t, x_sel[...])
+        grad_out_ref[...] += head_sums[:, layers + h : layers + h + 1] * gfh[h : h + 1, :]
 
     def layer(j, carried):
         jy, jc = j // 2, j % 2
@@ -438,7 +557,7 @@
 
         @pl.when(j > s)
         def _():
-            grad_out_ref[...] += mm(mm(act_t, values(1, j)).astype(bf16), gw_all[jy, jc], NT)
+            grad_out_ref[...] += mm(mm(act_t, values(1, j)).astype(bf16), gw_all[jy, jc])
 
         @pl.when(j < s)
         def _():
@@ -447,24 +566,21 @@
         return carried
 
     lax.fori_loop(0, layers, layer, 0)
-    grad_in_ref[...] = (turned[...] * scale_ref[...]).T
+    grad_in_ref[...] = (turned[...] * gain_ref[:, columns]).T
     loss = jnp.sum(jnp.where(lane == layers + heads, scal, 0.0), axis=0, keepdims=True)
-    loss_ref[...] = jnp.broadcast_to(jnp.sum(loss, axis=1, keepdims=True) / total, loss_ref.shape)
+    loss_ref[0, 0] = jnp.sum(loss) / total
     for copy in issued:
         copy.wait_send()
 
 
-def recurrence(layers, width, grad_scale, heads, tile, rows_ref, side_ref, out_ref):
+def recurrence(layers, width, grad_scale, tile, rows_ref, mask, target, coef, out_ref):
     adapt = 256
-    own = side_ref.shape[0]
+    heads = len(target)
+    own = mask.shape[0]
     sums = rows_ref[0, :own, 2 * adapt :]
-    side = side_ref[...]
     part = lambda k: sums[:, k : k + 1] + sums[:, 1 + heads + k : 2 + heads + k]
     sq = part(0)
     est = [part(1 + k) for k in range(heads)]
-    mask = side[:, 0:1]
-    target = [side[:, 1 + k : 2 + k] for k in range(heads)]
-    coef = [side[:, 4 + k : 5 + k] for k in range(heads)]
     into = [rows_ref[k, :own, :adapt] for k in range(layers)]
     onto = [rows_ref[k, :own, adapt : 2 * adapt] for k in range(layers)]
     head_out = [
@@ -544,80 +660,14 @@
 ):
     shards = lax.axis_size("dp")
     layers = lax.axis_size("section")
-    d = lax.axis_index("dp")
-    l = lax.axis_index("section")
     micro, cap, width = hidden.shape
     heads = value_heads.shape[0]
     adapt = weight_in.shape[2]
     total = micro * BAL * shards
     part = width // shards
     own = total // (shards * layers)
-    per_micro = total // micro
-
-    gain = norm_gain[0]
-    scale_sl = lax.dynamic_slice(gain, (d * part,), (part,))
-    gw_sl = lax.dynamic_slice(weight_in[0], (d * part, 0), (part, adapt))
-    gw_sl = (scale_sl[:, None] * gw_sl.astype(f32)).astype(bf16)
-
-    gfh = final_gain * value_heads
-    head_sl = lax.dynamic_slice(gfh, (0, d * part), (heads, part))
-    head_sl = jnp.concatenate([head_sl, jnp.zeros((8 - heads, part), f32)], axis=0)
-    terms = jnp.stack(split(gfh, 3), axis=1).reshape(3 * heads, width)
-    x0 = jnp.concatenate(
-        [
-            hidden.reshape(micro * cap, width),
-            terms,
-            jnp.zeros((128 - 3 * heads, width), bf16),
-        ],
-        axis=0,
-    )
-    ends = jnp.cumsum(lengths, axis=1)
-    begins = ends - lengths
-    offsets = jnp.arange(cap, dtype=jnp.int32)
-    batches = jnp.arange(micro, dtype=jnp.int32)
-    most = 3
-    begin = jnp.take(begins, d, axis=1)[:, None]
-    p = begin + offsets[None]
-    n = p // shards - (begin - p % shards + shards - 1) // shards
-    slot = (p % shards) * 16 + batches[:, None] * most + n
-    slot = jnp.where(offsets[None] < jnp.take(lengths, d, axis=1)[:, None], slot, -1).reshape(-1)
-    put = (jnp.arange(shards * 16, dtype=jnp.int32)[:, None] == slot[None]).astype(bf16)
-    q = (begins - d + shards - 1) // shards
-    p = d + shards * (q[:, :, None] + jnp.arange(most, dtype=jnp.int32))
-    seat = (2 * batches[:, None, None] + p // 128) * own + (p // shards) % own
-    seat = jnp.where(p < ends[:, :, None], seat, -1)
-    seat = jnp.swapaxes(seat, 0, 1).reshape(shards, micro * most)
-    seat = jnp.pad(seat, ((0, 0), (0, 16 - micro * most)), constant_values=-1).reshape(-1)
-    sel = (jnp.arange(layers * own, dtype=jnp.int32)[:, None] == seat[None]).astype(bf16)
-
-    token = jnp.where(
-        offsets[None, None, :] < lengths[:, :, None],
-        begins[:, :, None] + offsets[None, None, :],
-        -1,
-    )
-    batch = l // 2
-    ids = (l % 2) * 128 + shards * jnp.arange(own, dtype=jnp.int32) + d
-    spot = lax.dynamic_index_in_dim(token, batch, 0, keepdims=False).reshape(-1)
-    pick = (ids[:, None] == spot[None, :]).astype(f32)
-    used = lax.dynamic_index_in_dim(response_mask, batch, 0, keepdims=False).astype(f32)
-    aims = lax.dynamic_index_in_dim(old_values + advantages, batch, 1, keepdims=False)
-    mask = jnp.sum(pick * used[None, :], axis=1, keepdims=True)
-    aim = jnp.sum(pick[:, None, :] * aims[None], axis=2)
-    coef = jnp.concatenate([jnp.ones((1,), f32), multipliers])
-    side = jnp.concatenate(
-        [
-            mask,
-            aim,
-            jnp.broadcast_to(coef[None], (own, heads)),
-            jnp.zeros((own, 127 - 2 * heads), f32),
-        ],
-        axis=1,
-    )
-
-    place = (batches[:, None, None] * shards + token % shards) * 16 + token // 128 * own
-    place = jnp.where(token >= 0, place + token // shards % own, -1)
-    place = jnp.swapaxes(place, 0, 1).reshape(1, -1)
-
+
+    sm = pl.BlockSpec(memory_space=pltpu.SMEM)
     vm = pl.BlockSpec(memory_space=pltpu.VMEM)
     hbm = pl.BlockSpec(memory_space=pl.ANY)
     columns = layers * adapt + 128
@@ -628,18 +678,23 @@
         out_shape=(
             jax.ShapeDtypeStruct((part, adapt), f32),
             jax.ShapeDtypeStruct((adapt, part), f32),
-            jax.ShapeDtypeStruct((8, 128), f32),
+            jax.ShapeDtypeStruct((1, 1), f32),
         ),
-        in_specs=[hbm, hbm] + [vm] * 9,
-        out_specs=(vm, vm, vm),
+        in_specs=[sm, sm, hbm, hbm] + [vm] * 7,
+        out_specs=(vm, vm, sm),
         scratch_shapes=[
             pltpu.VMEM((shards, part, adapt), bf16),
             pltpu.VMEM((shards, adapt, part), bf16),
-            pltpu.VMEM((x0.shape[0], wide), f32),
+            pltpu.VMEM((micro * cap + 32, 2 * adapt), f32),
+            pltpu.VMEM((micro * cap, 32), f32),
+            pltpu.VMEM((micro * cap, part), f32),
+            pltpu.VMEM((32, part), f32),
+            pltpu.VMEM((micro, 1, shards * cap), jnp.int32),
+            pltpu.VMEM((shards * cap, part // 2), f32),
             pltpu.VMEM((SIDE, 2, adapt, part), bf16),
-            pltpu.VMEM((SIDE, 2, part, adapt), bf16),
-            pltpu.VMEM((2, shards, micro * cap, part // 2), bf16),
-            pltpu.VMEM((total, part), bf16),
+            pltpu.VMEM((SIDE, 2, adapt, part), bf16),
+            pltpu.VMEM((2, shards, micro, cap, part // 2), bf16),
+            pltpu.VMEM((2, total, part // 2), bf16),
             pltpu.VMEM((2, SIDE, SIDE, SIDE, 16, columns), bf16),
             pltpu.VMEM((shards, 16, wide), bf16),
             pltpu.VMEM((SIDE, SIDE, 16, layers * adapt), bf16),
@@ -666,17 +721,17 @@
         ),
         name="layers",
     )(
+        lengths,
+        multipliers,
         weight_in[0],
         weight_out[0],
-        gw_sl,
-        gain[None],
-        x0,
-        put,
-        sel,
-        side,
-        place,
-        head_sl,
-        scale_sl[None],
+        norm_gain,
+        hidden,
+        final_gain[None],
+        value_heads,
+        response_mask,
+        old_values,
+        advantages,
     )
     return (grad_in[None], grad_out[None], loss[0, 0])
 

time: 155 us -> 131 us (0.85)
  other arithmetic: 12.7 us -> 0 us
  Pallas kernels: 128 us -> 120 us
  local copies, waits for them, and re-layouts: 13.2 us -> 8.25 us
  between operations: 0.8 us -> 2.46 us
    pallas_call x1, Pallas kernels: 128 us -> 120 us  [local(): pl.pallas_call(functools.partial(kernel, layers, float(width), LOSS_SCALE...]
    concatenate x3 -> x0, other arithmetic: 5.12 us -> none  [the longest x1 4.38 us: local(): jnp.concatenate([hidden.reshape(micro * cap, width), terms, jnp.zeros((12...]
    convert_element_type x5 -> x0, other arithmetic: 3.89 us -> none  [the longest x1 1.79 us: local(): gw_sl = (scale_sl[:, None] * gw_sl.astype(f32)).astype(bf16)]
    reshape x2 -> x0, local copies, waits for them, and re-layouts: 1.89 us -> none  [the longest x1 1.75 us: local(): hidden.reshape(micro * cap, width)]
    unnamed x11 -> x3, local copies, waits for them, and re-layouts: 6.82 us -> 8.25 us
where the time goes in v1:
time: 131 us
  Pallas kernels  120 us (92%)
  local copies, waits for them, and re-layouts  8.25 us (6%)
  between operations  2.46 us (2%)
    pallas_call x1, Pallas kernels, local(): pl.pallas_call(functools.partial(kernel, layers, float(width), LOSS_SCALE...  120 us
    unnamed x3, local copies, waits for them, and re-layouts  8.25 us

profile of v1, /device:TPU:1, one launch (start us, length us, event | category | flops | bytes accessed | tf_op | source)
XLA Modules:
  0.0 130.6 jit_solution(5351775300182451665)
XLA Ops:
  0.6 4.5 %copy.14.hid_ref = bf16[4,36,8192]{2,1,0:T(8,128)(2,1)} copy(bf16[4,36,8192]{2,0,1:T(4,128)(2,1)} %param.11) | data formatting | bytes 4718592 | tf_op args[0]
  5.1 119.9 %layers.1 = (f32[512,256]{1,0:T(8,128)}, f32[256,512]{1,0:T(8,128)}, f32[1,1]{1,0:T(1,128)}) custom-call(s32[4,16]{1,0:T(4,128)} %lengths_ref.1, f32[2]{0:T(128)} %coef_ref.1, bf16[8192,256]{1,0:T(8,128)(2,1)} %bitcast.8, bf16[256,8192]{1,0:T(8,128)(2,1)} %bitcast.9, f32[1,8192]{1,0:T(1,128)} %gain_ref.1, bf16[4,36,8192]{2,1,0:T(8,128)(2,1)} %copy.14.hid_ref, ...), custom_call_target="tpu_custom_call" | custom-call | flops 10000000000 | bytes 30000000 | tf_op jit(solution)/shard_map/layers/pallas_call | solution.py:676
  125.0 1.9 %copy.18 = f32[1,512,256]{2,1,0:T(8,128)} copy(f32[1,512,256]{2,1,0:T(8,128)} %bitcast.7) | data formatting | bytes 1048576
  126.9 1.9 %copy.19 = f32[1,256,512]{2,1,0:T(8,128)} copy(f32[1,256,512]{2,1,0:T(8,128)} %bitcast.6) | data formatting | bytes 1048576

commit v2 on v1

--- a/solution.py
+++ b/solution.py
@@ -47,12 +47,10 @@
     wout,
     sums,
     est,
-    xf,
     terms,
     tokens_at,
     xm,
-    wo_all,
-    gw_all,
+    weights,
     x_all,
     x_sel,
     pay,
@@ -68,7 +66,9 @@
     mine,
     other,
     block,
-    sums_t,
+    acc,
+    both_t,
+    scal_t,
     send_sem,
     recv_sem,
     local_sem,
@@ -81,7 +81,7 @@
     shards = SIDE * SIDE
     chunks, part, adapt = win.shape
     heads = head_ref.shape[0]
-    micro, cap = hid_ref.shape[:2]
+    cap, micro = hid_ref.shape[:2]
     rows = micro * cap
     step = lambda a, off: (me[a] + off + SIDE) % SIDE
 
@@ -270,6 +270,8 @@
         for (p, row, v), at_ in swaps.items():
             arrived(ref(p, 1 - c, None, row, v), at_)
 
+    wo_all, gw_all = weights.at[0], weights.at[1]
+
     chunks = win.shape[0]
     loads = []
     for k in range(chunks):
@@ -317,12 +319,11 @@
             at = at + length[m][i]
         mine_at.append(here)
     lane = lax.broadcasted_iota(jnp.int32, (1, rows), 1)
-    m_of, b_of, n_of = jnp.zeros_like(lane), jnp.zeros_like(lane), jnp.zeros_like(lane)
+    b_of, n_of = jnp.zeros_like(lane), jnp.zeros_like(lane)
+    m_of, r_of = lane & 3, lane >> 2
     for m in range(micro):
-        m_of = jnp.where(lane >= m * cap, m, m_of)
-        b_of = jnp.where(lane >= m * cap, mine_at[m], b_of)
-        n_of = jnp.where(lane >= m * cap, lengths_ref[m, d], n_of)
-    r_of = lane - m_of * cap
+        b_of = jnp.where(m_of == m, mine_at[m], b_of)
+        n_of = jnp.where(m_of == m, lengths_ref[m, d], n_of)
     p = b_of + r_of
     n = (p >> 4) - ((b_of - (p & 15) + 15) >> 4)
     slot = jnp.where(r_of < n_of, (p & 15) * 16 + m_of * 3 + n, -1)
@@ -358,12 +359,24 @@
             first_lane = jnp.where(lane >= i * cap, i * cap, first_lane)
         row = lane - first_lane
         row = jnp.where(row < e, b + row, -1)
-        tokens_at[m] = row
         spot = jnp.where(batch == m, row, spot)
         used = jnp.where(batch == m, mask_ref[m : m + 1, :].astype(f32), used)
         for h in range(heads):
             aim = old_ref[h, m : m + 1, :] + adv_ref[h, m : m + 1, :]
             aims[h] = jnp.where(batch == m, aim, aims[h])
+    lane = lax.broadcasted_iota(jnp.int32, (1, shards * rows), 1)
+    b_of, n_of, src = jnp.zeros_like(lane), jnp.zeros_like(lane), jnp.zeros_like(lane)
+    for i in range(shards):
+        src = jnp.where(lane >= i * rows, i, src)
+    for m in range(micro):
+        b, e = jnp.zeros_like(lane), jnp.zeros_like(lane)
+        for i in range(shards):
+            b = jnp.where(src == i, begin[m][i] + 256 * m, b)
+            e = jnp.where(src == i, length[m][i], e)
+        b_of = jnp.where((lane & 3) == m, b, b_of)
+        n_of = jnp.where((lane & 3) == m, e, n_of)
+    row = (lane - src * rows) >> 2
+    tokens_at[...] = jnp.where(row < n_of, b_of + row, -1)
     pick = ids == spot
     mask = jnp.sum(jnp.where(pick, used, 0.0), axis=1, keepdims=True)
     target = [jnp.sum(jnp.where(pick, aim, 0.0), axis=1, keepdims=True) for aim in aims]
@@ -377,14 +390,12 @@
 
     def chunk(k, square):
         cut = pl.ds(pl.multiple_of(k * part, part), part)
-        for m in range(micro):
-            xf[m * cap : (m + 1) * cap, :] = hid_ref[m, :, cut].astype(f32)
+        x = hid_ref[:, :, cut].astype(f32).reshape(rows, part)
         left = final_ref[:, cut] * head_ref[:, cut]
         for t in range(3):
             term = left.astype(bf16).astype(f32)
             terms[8 * t : 8 * t + heads, :] = term
             left = left - term
-        x = xf[...]
         for i in range(part // 128):
             piece = x[:, i * 128 : (i + 1) * 128]
             square = square + piece * piece
@@ -504,16 +515,18 @@
         for copy in keep:
             copy.wait()
         quarter = x_sel.shape[1] // micro
-        at = lax.broadcasted_iota(jnp.int32, (quarter, shards * cap), 0)
+        for h in (0, 1):
+            for src in range(shards):
+                block_in = x_all[h, src].astype(f32).reshape(rows, wide)
+                xm[h, src * rows : (src + 1) * rows, :] = block_in.astype(bf16)
+        at = lax.broadcasted_iota(jnp.int32, (quarter, 1), 0)
         token = ((at >> 3) & 1) * 128 + (at & 7) * 16 + (at >> 4)
 
         def batch(i, carried):
             m, h = i // 2, i % 2
-            for src in range(shards):
-                xm[src * cap : (src + 1) * cap, :] = x_all[h, src, m].astype(f32)
-            seat = jnp.where(token == tokens_at[m], 1.0, 0.0).astype(bf16)
+            seat = jnp.where(token + m * 256 == tokens_at[...], 1.0, 0.0).astype(bf16)
             start = pl.multiple_of(m * quarter, quarter)
-            x_sel[h, pl.ds(start, quarter), :] = mm(seat, xm[...].astype(bf16)).astype(bf16)
+            x_sel[h, pl.ds(start, quarter), :] = mm(seat, xm[h]).astype(bf16)
             return carried
 
         lax.fori_loop(0, 2 * micro, batch, 0)
@@ -533,40 +546,35 @@
     def lanes(kind):
         return pay[kind, :, :, :, :, layers * adapt :].reshape(total, 128)
 
-    act_t = values(0, s).T
-    delta_t = values(1, s).T
     scal = lanes(0).astype(f32) + lanes(1).astype(f32)
     lane = lax.broadcasted_iota(jnp.int32, (total, 128), 1)
-    sigma = jnp.sum(jnp.where(lane == s, scal, 0.0), axis=1, keepdims=True)
+    scal_t[...] = scal.T
+    both_t[0] = values(0, s).T
+    both_t[1] = values(1, s).T
+    act_t, delta_t = both_t[0], both_t[1]
     head_sums = mm(act_t, lanes(0)) + mm(act_t, lanes(1))
-    turned = sums_t
+    wide_t = act_t.astype(f32)
+
+    def scaled(at):
+        return (wide_t * -scal_t[pl.ds(at, 1), :]).astype(bf16)
+
+    own_t = scaled(s)
+    gfh = final_ref[:, columns] * head_ref[:, columns]
     for n in (0, 1):
         cut = slice(n * wide, (n + 1) * wide)
-        grad_out_ref[:, cut] = -mm(act_t, (x_sel[n].astype(f32) * sigma).astype(bf16))
-        turned[:, cut] = mm(delta_t, x_sel[n])
-    gfh = final_ref[:, columns] * head_ref[:, columns]
-    for h in range(heads):
-        grad_out_ref[...] += head_sums[:, layers + h : layers + h + 1] * gfh[h : h + 1, :]
-
-    def layer(j, carried):
-        jy, jc = j // 2, j % 2
-        by = jnp.sum(jnp.where(lane == jnp.maximum(j, s), scal, 0.0), axis=1, keepdims=True)
-        acts = values(0, j)
-        scaled = (acts.astype(f32) * -by).astype(bf16)
-        grad_out_ref[...] += mm(mm(act_t, scaled).astype(bf16), wo_all[jy, jc])
-
-        @pl.when(j > s)
-        def _():
-            grad_out_ref[...] += mm(mm(act_t, values(1, j)).astype(bf16), gw_all[jy, jc])
-
-        @pl.when(j < s)
-        def _():
-            turned[...] += mm(mm(delta_t, acts).astype(bf16), wo_all[jy, jc])
-
-        return carried
-
-    lax.fori_loop(0, layers, layer, 0)
-    grad_in_ref[...] = (turned[...] * gain_ref[:, columns]).T
+        out = mm(own_t, x_sel[n])
+        for h in range(heads):
+            out = out + head_sums[:, layers + h : layers + h + 1] * gfh[h : h + 1, cut]
+        acc[0, :, cut] = out
+        acc[1, :, cut] = mm(delta_t, x_sel[n])
+    for j in range(layers):
+        which = jnp.where(j > s, 0, 1)
+        left = mm(scaled(jnp.maximum(j, s)), values(0, j)).astype(bf16)
+        right = mm(both_t[which], values(1 - which, j)).astype(bf16)
+        acc[0] += mm(left, wo_all[j // 2, j % 2])
+        acc[jnp.where(j == s, 2, which)] += mm(right, weights[1 - which, j // 2, j % 2])
+    grad_out_ref[...] = acc[0]
+    grad_in_ref[...] = (acc[1] * gain_ref[:, columns]).T
     loss = jnp.sum(jnp.where(lane == layers + heads, scal, 0.0), axis=0, keepdims=True)
     loss_ref[0, 0] = jnp.sum(loss) / total
     for copy in issued:
@@ -645,6 +653,11 @@
     out_ref[1, :, layers * adapt :] = extra - high
 
 
+def results(grad_in_ref, grad_out_ref, in_ref, out_ref):
+    in_ref[...] = grad_in_ref[...]
+    out_ref[...] = grad_out_ref[...]
+
+
 def local(
     hidden,
     lengths,
@@ -687,13 +700,11 @@
             pltpu.VMEM((shards, adapt, part), bf16),
             pltpu.VMEM((micro * cap + 32, 2 * adapt), f32),
             pltpu.VMEM((micro * cap, 32), f32),
-            pltpu.VMEM((micro * cap, part), f32),
             pltpu.VMEM((32, part), f32),
-            pltpu.VMEM((micro, 1, shards * cap), jnp.int32),
-            pltpu.VMEM((shards * cap, part // 2), f32),
-            pltpu.VMEM((SIDE, 2, adapt, part), bf16),
-            pltpu.VMEM((SIDE, 2, adapt, part), bf16),
-            pltpu.VMEM((2, shards, micro, cap, part // 2), bf16),
+            pltpu.VMEM((1, shards * micro * cap), jnp.int32),
+            pltpu.VMEM((2, shards * micro * cap, part // 2), bf16),
+            pltpu.VMEM((2, SIDE, 2, adapt, part), bf16),
+            pltpu.VMEM((2, shards, cap, micro, part // 2), bf16),
             pltpu.VMEM((2, total, part // 2), bf16),
             pltpu.VMEM((2, SIDE, SIDE, SIDE, 16, columns), bf16),
             pltpu.VMEM((shards, 16, wide), bf16),
@@ -708,7 +719,9 @@
             pltpu.VMEM((2, own, columns), f32),
             pltpu.VMEM((own, columns), f32),
             pltpu.VMEM((16, columns), bf16),
-            pltpu.VMEM((adapt, part), f32),
+            pltpu.VMEM((3, adapt, part), f32),
+            pltpu.VMEM((2, adapt, total), bf16),
+            pltpu.VMEM((128, total), f32),
             pltpu.SemaphoreType.DMA((COPIES,)),
             pltpu.SemaphoreType.DMA((COPIES,)),
             pltpu.SemaphoreType.DMA((40,)),
@@ -726,13 +739,23 @@
         weight_in[0],
         weight_out[0],
         norm_gain,
-        hidden,
+        jnp.swapaxes(hidden, 0, 1),
         final_gain[None],
         value_heads,
         response_mask,
         old_values,
         advantages,
     )
+    grad_in, grad_out = pl.pallas_call(
+        results,
+        out_shape=(
+            jax.ShapeDtypeStruct(grad_in.shape, f32),
+            jax.ShapeDtypeStruct(grad_out.shape, f32),
+        ),
+        in_specs=[vm, vm],
+        out_specs=(vm, vm),
+        name="results",
+    )(grad_in, grad_out)
     return (grad_in[None], grad_out[None], loss[0, 0])
 
 

time: 131 us -> 118 us (0.901)
  local copies, waits for them, and re-layouts: 8.25 us -> 0 us
  Pallas kernels: 120 us -> 115 us
    unnamed x3 -> x0, local copies, waits for them, and re-layouts: 8.25 us -> none
    pallas_call x1, Pallas kernels: 120 us -> 113 us  [local(): pl.pallas_call(functools.partial(kernel, layers, float(width), LOSS_SCALE...]
    pallas_call x0 -> x1, Pallas kernels: none -> 2.2 us  [local(): pl.pallas_call(results, out_shape=(jax.ShapeDtypeStruct(grad_in.shape, f3...]
where the time goes in v2:
time: 118 us; the launch traced here: 117 us
  Pallas kernels  115 us (97%)
  between operations  2.41 us (2%)
    pallas_call x1, Pallas kernels, local(): pl.pallas_call(functools.partial(kernel, layers, float(width), LOSS_SCALE...  113 us

profile of v2, /device:TPU:1, one launch (start us, length us, event | category | flops | bytes accessed | tf_op | source)
XLA Modules:
  0.0 117.3 jit_solution(10903788129462321469)
XLA Ops:
  0.6 112.7 %layers.1 = (f32[512,256]{1,0:T(8,128)}, f32[256,512]{1,0:T(8,128)}, f32[1,1]{1,0:T(1,128)}) custom-call(s32[4,16]{1,0:T(4,128)} %lengths_ref.1, f32[2]{0:T(128)} %coef_ref.1, bf16[8192,256]{1,0:T(8,128)(2,1)} %bitcast.7, bf16[256,8192]{1,0:T(8,128)(2,1)} %bitcast.8, f32[1,8192]{1,0:T(1,128)} %gain_ref.1, bf16[36,4,8192]{2,1,0:T(4,128)(2,1)} %bitcast.9, ...), custom_call_target="tpu_custom_call" | custom-call | flops 10000000000 | bytes 30000000 | tf_op jit(solution)/shard_map/layers/pallas_call | solution.py:689
  113.4 2.2 %results.1 = (f32[512,256]{1,0:T(8,128)}, f32[256,512]{1,0:T(8,128)}) custom-call(f32[512,256]{1,0:T(8,128)} %get-tuple-element.8.grad_in_ref, f32[256,512]{1,0:T(8,128)} %get-tuple-element.9.grad_out_ref), custom_call_target="tpu_custom_call" | custom-call | tf_op jit(solution)/shard_map/results/pallas_call | solution.py:749

commit v3 on v2

--- a/solution.py
+++ b/solution.py
@@ -33,6 +33,16 @@
     coef_ref,
     win_ref,
     wout_ref,
+    gain_in,
+    hid_in,
+    final_in,
+    head_in,
+    mask_in,
+    old_in,
+    adv_in,
+    grad_in_ref,
+    grad_out_ref,
+    loss_ref,
     gain_ref,
     hid_ref,
     final_ref,
@@ -40,9 +50,6 @@
     mask_ref,
     old_ref,
     adv_ref,
-    grad_in_ref,
-    grad_out_ref,
-    loss_ref,
     win,
     wout,
     sums,
@@ -100,17 +107,6 @@
     def layer_at(off):
         return (s + off + layers) % layers
 
-    barrier = pltpu.get_barrier_semaphore()
-    for off in range(1, shards):
-        pl.semaphore_signal(
-            barrier, inc=1, device_id={"section": s, "dp": shard_at(off)}, device_id_type=MESH
-        )
-    for off in range(1, layers):
-        pl.semaphore_signal(
-            barrier, inc=1, device_id={"section": layer_at(off), "dp": d}, device_id_type=MESH
-        )
-    pl.semaphore_wait(barrier, shards + layers - 2)
-
     issued = []
     count = [0, 0]
 
@@ -193,7 +189,7 @@
                 arrived(self.slab(v, h, 1 - c), at)
 
     def gather(at, columns, meanwhile=None):
-        third = (columns // 384) * 128
+        third = (columns + 192) // 384 * 128
         bounds = [0, third, 2 * third, columns]
         orders = [("x", "z", "y"), ("z", "y", "x"), ("y", "x", "z")]
         parts = range(3)
@@ -271,20 +267,43 @@
             arrived(ref(p, 1 - c, None, row, v), at_)
 
     wo_all, gw_all = weights.at[0], weights.at[1]
-
-    chunks = win.shape[0]
+    columns = pl.ds(pl.multiple_of(d * part, part), part)
+    own_wo = local(wout_ref.at[:, columns], wo_all.at[y, c])
+    own_hid = local(hid_in, hid_ref)
+    small = [
+        local(src, dst)
+        for src, dst in (
+            (gain_in, gain_ref),
+            (final_in, final_ref),
+            (head_in, head_ref),
+            (mask_in, mask_ref),
+            (old_in, old_ref),
+            (adv_in, adv_ref),
+        )
+    ]
     loads = []
     for k in range(chunks):
         loads.append(local(win_ref.at[pl.ds(k * part, part)], win.at[k]))
         loads.append(local(wout_ref.at[:, pl.ds(k * part, part)], wout.at[k]))
 
+    barrier = pltpu.get_barrier_semaphore()
+    for off in range(1, shards):
+        pl.semaphore_signal(
+            barrier, inc=1, device_id={"section": s, "dp": shard_at(off)}, device_id_type=MESH
+        )
+    for off in range(1, layers):
+        pl.semaphore_signal(
+            barrier, inc=1, device_id={"section": layer_at(off), "dp": d}, device_id_type=MESH
+        )
+    pl.semaphore_wait(barrier, shards + layers - 2)
+
     half = adapt // 2
     wo_ring = Ring(
         "y", lambda v, h, core: wo_all.at[step("y", v), core, pl.ds(h * half, half)], True
     )
-    columns = pl.ds(pl.multiple_of(d * part, part), part)
-    local(wout_ref.at[:, columns], wo_all.at[y, c]).wait()
+    own_wo.wait()
     wo_ring.start()
+    own_hid.wait()
     wide = part // 2
     keep = []
     for h in (0, 1):
@@ -307,6 +326,9 @@
     gw_ring = Ring(
         "y", lambda v, h, core: gw_all.at[step("y", v), core, pl.ds(h * half, half)], True
     )
+
+    for copy in small:
+        copy.wait()
 
     begin = [[None] * shards for _ in range(micro)]
     length = [[lengths_ref[m, i] for i in range(shards)] for m in range(micro)]
@@ -693,9 +715,16 @@
             jax.ShapeDtypeStruct((adapt, part), f32),
             jax.ShapeDtypeStruct((1, 1), f32),
         ),
-        in_specs=[sm, sm, hbm, hbm] + [vm] * 7,
+        in_specs=[sm, sm] + [hbm] * 9,
         out_specs=(vm, vm, sm),
         scratch_shapes=[
+            pltpu.VMEM((1, width), f32),
+            pltpu.VMEM((cap, micro, width), bf16),
+            pltpu.VMEM((1, width), f32),
+            pltpu.VMEM((heads, width), f32),
+            pltpu.VMEM(response_mask.shape, jnp.int32),
+            pltpu.VMEM(old_values.shape, f32),
+            pltpu.VMEM(advantages.shape, f32),
             pltpu.VMEM((shards, part, adapt), bf16),
             pltpu.VMEM((shards, adapt, part), bf16),
             pltpu.VMEM((micro * cap + 32, 2 * adapt), f32),
@@ -724,7 +753,7 @@
             pltpu.VMEM((128, total), f32),
             pltpu.SemaphoreType.DMA((COPIES,)),
             pltpu.SemaphoreType.DMA((COPIES,)),
-            pltpu.SemaphoreType.DMA((40,)),
+            pltpu.SemaphoreType.DMA((48,)),
         ],
         compiler_params=pltpu.CompilerParams(
             vmem_limit_bytes=60 * 1024 * 1024, collective_id=0, has_side_effects=True

time: 118 us -> 112 us (0.949)
  Pallas kernels: 115 us -> 110 us
    pallas_call x1, Pallas kernels: 113 us -> 108 us  [local(): pl.pallas_call(functools.partial(kernel, layers, float(width), LOSS_SCALE...]
where the time goes in v3:
time: 112 us
  Pallas kernels  110 us (98%)
  between operations  2.41 us (2%)
    pallas_call x1, Pallas kernels, local(): pl.pallas_call(functools.partial(kernel, layers, float(width), LOSS_SCALE...  108 us

profile of v3, /device:TPU:1, one launch (start us, length us, event | category | flops | bytes accessed | tf_op | source)
XLA Modules:
  0.0 112.2 jit_solution(7115086438264938892)
XLA Ops:
  0.6 107.5 %layers.1 = (f32[512,256]{1,0:T(8,128)}, f32[256,512]{1,0:T(8,128)}, f32[1,1]{1,0:T(1,128)}) custom-call(s32[4,16]{1,0:T(4,128)} %lengths_ref.1, f32[2]{0:T(128)} %coef_ref.1, bf16[8192,256]{1,0:T(8,128)(2,1)} %bitcast.7, bf16[256,8192]{1,0:T(8,128)(2,1)} %bitcast.8, f32[1,8192]{1,0:T(1,128)} %gain_in.1, bf16[36,4,8192]{2,1,0:T(4,128)(2,1)} %bitcast.9, ...), custom_call_target="tpu_custom_call" | custom-call | flops 10000000000 | bytes 30000000 | tf_op jit(solution)/shard_map/layers/pallas_call | solution.py:711
  108.2 2.2 %results.1 = (f32[512,256]{1,0:T(8,128)}, f32[256,512]{1,0:T(8,128)}) custom-call(f32[512,256]{1,0:T(8,128)} %get-tuple-element.8.grad_in_ref, f32[256,512]{1,0:T(8,128)} %get-tuple-element.9.grad_out_ref), custom_call_target="tpu_custom_call" | custom-call | tf_op jit(solution)/shard_map/results/pallas_call | solution.py:778
